TPU v7x, 32 devices: a whole 2x2x4 slice. The times are simulated.
32 devices in a mesh: band: 2 (over x), grow: 4 (over z), gcol: 4 (over y, core).
Axes of the slice: x: 2, y: 2, z: 4, core: 2. Of those that a mesh axis runs over, the one named last changes fastest.
Arguments:
- valence: bfloat16 [4, 110592], replicated, may hold values from -6 to 6
- conduction: bfloat16 [32, 110592], P(('band', 'grow', 'gcol')), may hold values from -6 to 6
- val_energy: float32 [4], replicated, may hold values from -1 to 0
- cond_energy: float32 [32], replicated, may hold values from 0.2 to 3
- frequencies: float32 [2], replicated, may hold values from 0.1 to 2
- gvec_index: int32 [2048], replicated, may hold values from 0 to 110591, as said below
- first_band: int32 [4], replicated, may hold values from 0 to 15
Outputs:
- chi_zero: bfloat16 [2048, 2, 2, 2048], P(('grow', 'band'), None, None, 'gcol')
Inputs may be any that keep to these rules, and one draw needn't show every extreme that they name: `gvec_index`: all 2048 entries are different.
All inputs are finite; a program needn't handle non-finite values.
Results may differ from a plain program's by a relative error of at most 0.0059.
Values may be sent and summed in bfloat16 or wider, within the bound.
A program may use at most 128 MiB of HBM per device.

v0:
```python
import functools
import math

import jax
import jax.numpy as jnp
import ml_dtypes
import numpy as np
from jax import lax
from jax.experimental import pallas as pl
from jax.experimental.pallas import tpu as pltpu
from jax.sharding import PartitionSpec as P

GRID = 48
HALF = GRID // 2 + 1
PLANE = GRID * GRID
CHUNK = 256
CHUNKS = -(-GRID * HALF // CHUNK)
TILE = 256
LANES = 128
MESH = pl.DeviceIdType.MESH
TABLE_SCALE = 1.622
TABLE_GAIN = 1.6242055647


def plane_table():
    line = np.arange(GRID)
    k2, k3 = np.meshgrid(line, np.arange(HALF), indexing="ij")
    k2, k3 = k2.reshape(-1), k3.reshape(-1)
    b, e = np.meshgrid(line, line, indexing="ij")
    b, e = b.reshape(-1), e.reshape(-1)
    turn = (b[:, None] * k2[None] + e[:, None] * k3[None]) % GRID
    angle = 2.0 * np.pi * line / GRID
    parts = []
    for values in (np.cos(angle), -np.sin(angle)):
        small = (values * TABLE_SCALE).astype(np.float32).astype(ml_dtypes.bfloat16)
        full = np.zeros((PLANE, CHUNKS * CHUNK), ml_dtypes.bfloat16)
        full[:, : GRID * HALF] = small[turn]
        parts.append(full.reshape(PLANE, CHUNKS, CHUNK).transpose(1, 0, 2))
    return np.concatenate(parts, 0)


def phase_table():
    line = np.arange(GRID)
    angle = 2.0 * np.pi * (line[:, None] * line[None] % GRID) / GRID
    scale = GRID ** (-1.5) / TABLE_GAIN
    both = np.zeros((2 * GRID, LANES), np.float32)
    both[:, :GRID] = np.concatenate([np.cos(angle), np.sin(angle)], 0) * scale
    high = both.astype(ml_dtypes.bfloat16)
    low = (both - high.astype(np.float32)).astype(ml_dtypes.bfloat16)
    return np.concatenate([high, low], 0)


def density_kernel(val_ref, cond_ref, table_ref, phase_ref, index_ref, out_ref, pair, planes):
    step = pl.program_id(0)
    rows = val_ref.shape[0]
    pairs = rows // GRID
    num_tiles = out_ref.shape[0]

    @pl.when(step == 0)
    def _():
        cond = cond_ref[...].astype(jnp.float32)
        for v in range(pairs):
            product = val_ref[v * GRID : (v + 1) * GRID].astype(jnp.float32) * cond
            high = product.astype(jnp.bfloat16)
            pair[v * GRID : (v + 1) * GRID] = high
            pair[rows + v * GRID : rows + (v + 1) * GRID] = (
                product - high.astype(jnp.float32)
            ).astype(jnp.bfloat16)

    both = jnp.dot(pair[...], table_ref[0], preferred_element_type=jnp.float32)
    plane = both[:rows] + both[rows:]
    high = plane.astype(jnp.bfloat16)
    planes[step, :rows] = high
    planes[step, rows:] = (plane - high.astype(jnp.float32)).astype(jnp.bfloat16)

    @pl.when(step == 2 * CHUNKS - 1)
    def _():
        @pl.loop(0, num_tiles)
        def _(tile):
            index = index_ref[tile]
            index_float = index.astype(jnp.float32)
            upper = jnp.floor((index_float + 0.5) * (1.0 / GRID))
            k3 = index_float - GRID * upper
            k1 = jnp.floor((upper + 0.5) * (1.0 / GRID))
            k2 = upper - GRID * k1
            mirror = k3 > HALF - 1
            k1 = jnp.where(mirror & (k1 > 0), GRID - k1, k1).astype(jnp.int32)
            k2 = jnp.where(mirror & (k2 > 0), GRID - k2, k2)
            k3 = jnp.where(mirror, GRID - k3, k3)
            sign = jnp.where(mirror, -1.0, 1.0)
            place = (k2 * HALF + k3).astype(jnp.int32)
            real = jnp.zeros((2 * rows, TILE), jnp.float32)
            imag = jnp.zeros((2 * rows, TILE), jnp.float32)
            line = lax.broadcasted_iota(jnp.int32, (CHUNK, TILE), 0)
            for chunk in range(CHUNKS):
                pick = jnp.where(line == place - chunk * CHUNK, 1.0, 0.0).astype(jnp.bfloat16)
                real += jnp.dot(planes[chunk], pick, preferred_element_type=jnp.float32)
                imag += jnp.dot(planes[CHUNKS + chunk], pick, preferred_element_type=jnp.float32)
            real = (real[:rows] + real[rows:]).reshape(pairs, GRID, TILE)
            imag = (imag[:rows] + imag[rows:]).reshape(pairs, GRID, TILE)
            pick = jnp.where(line[:LANES] == k1, 1.0, 0.0).astype(jnp.bfloat16)
            phases = jnp.dot(phase_ref[...], pick, preferred_element_type=jnp.float32)
            phases = phases[: 2 * GRID] + phases[2 * GRID :]
            cos_one, sin_one = phases[:GRID], phases[GRID:]
            out_real = jnp.sum(real * cos_one + imag * sin_one, axis=1)
            out_imag = jnp.sum(imag * cos_one - real * sin_one, axis=1) * sign
            out = jnp.concatenate([out_real, out_imag], 0)
            out = jnp.concatenate([out[:, :LANES], out[:, LANES:]], 0)
            out_ref[tile] = out.astype(jnp.bfloat16)


def tile_density(valence, conduction, gvec_index):
    val_count = valence.shape[0]
    rows = val_count * GRID
    num_tiles = gvec_index.shape[0] // TILE
    whole = lambda *shape: pl.BlockSpec(shape, lambda n: (0,) * len(shape))
    return pl.pallas_call(
        density_kernel,
        grid=(2 * CHUNKS,),
        out_shape=jax.ShapeDtypeStruct((num_tiles, 4 * val_count, LANES), jnp.bfloat16),
        in_specs=[
            whole(rows, PLANE),
            whole(GRID, PLANE),
            pl.BlockSpec((1, PLANE, CHUNK), lambda n: (n, 0, 0)),
            whole(4 * GRID, LANES),
            whole(num_tiles, 1, TILE),
        ],
        out_specs=whole(num_tiles, 4 * val_count, LANES),
        scratch_shapes=[
            pltpu.VMEM((2 * rows, PLANE), jnp.bfloat16),
            pltpu.VMEM((2 * CHUNKS, 2 * rows, CHUNK), jnp.bfloat16),
        ],
        compiler_params=pltpu.CompilerParams(vmem_limit_bytes=48 * 2**20),
    )(
        valence.reshape(rows, PLANE),
        conduction.reshape(GRID, PLANE),
        jnp.asarray(plane_table()),
        jnp.asarray(phase_table()),
        gvec_index.reshape(num_tiles, 1, TILE),
    )


def device_of(number, sizes):
    band_count, grow_count, gcol_count = sizes
    return number // (grow_count * gcol_count), number // gcol_count % grow_count, number % gcol_count


def exchange_kernel(sizes, tiles_ref, weight_ref, out_ref, rows_in, cols_in, send_sem, recv_sem, own_sem):
    band_count, grow_count, gcol_count = sizes
    devices = band_count * grow_count * gcol_count
    num_tiles = tiles_ref.shape[0]
    col_tiles = num_tiles // gcol_count
    me = (lax.axis_index("band") * grow_count + lax.axis_index("grow")) * gcol_count + lax.axis_index("gcol")

    def row_tile(place):
        return (place[1] * band_count + place[0]) * num_tiles // (grow_count * band_count)

    barrier = pltpu.get_barrier_semaphore()

    @pl.loop(1, devices)
    def _(offset):
        place = device_of(lax.rem(me + offset, devices), sizes)
        pl.semaphore_signal(barrier, inc=1, device_id=place, device_id_type=MESH)

    pl.semaphore_wait(barrier, devices - 1)

    @pl.loop(1, devices)
    def _(offset):
        place = device_of(lax.rem(me + offset, devices), sizes)
        pltpu.make_async_remote_copy(
            tiles_ref.at[row_tile(place)], rows_in.at[me], send_sem.at[0], recv_sem.at[0],
            device_id=place, device_id_type=MESH,
        ).start()
        pltpu.make_async_remote_copy(
            tiles_ref.at[pl.ds(place[2] * col_tiles, col_tiles)], cols_in.at[me], send_sem.at[1], recv_sem.at[1],
            device_id=place, device_id_type=MESH,
        ).start()

    here = device_of(me, sizes)
    pltpu.make_async_copy(tiles_ref.at[row_tile(here)], rows_in.at[me], recv_sem.at[0]).start()
    pltpu.make_async_copy(
        tiles_ref.at[pl.ds(here[2] * col_tiles, col_tiles)], cols_in.at[me], recv_sem.at[1]
    ).start()
    pltpu.make_async_copy(rows_in, rows_in, recv_sem.at[0]).wait()
    pltpu.make_async_copy(cols_in, cols_in, recv_sem.at[1]).wait()
    for held, sem in ((rows_in, 0), (cols_in, 1)):
        others = held.at[pl.ds(0, devices - 1)]
        pltpu.make_async_copy(others, others, send_sem.at[sem]).wait()

    cols = cols_in[...].astype(jnp.float32)
    half = cols.shape[2] // 2
    depth = devices * half
    right = jnp.concatenate(
        [cols[:, tile, side * half : (side + 1) * half].reshape(depth, LANES)
         for tile in range(col_tiles) for side in range(2)], 1
    ).astype(jnp.bfloat16)
    rows = rows_in[...].astype(jnp.float32)
    for side in range(2):
        part = rows[:, side * half : (side + 1) * half]
        for freq in range(out_ref.shape[0]):
            left = part * weight_ref[freq]
            swapped = jnp.concatenate([left[:, half // 2 :], -left[:, : half // 2]], 1)
            for kind, value in enumerate((left, swapped)):
                value = value.reshape(depth, LANES).astype(jnp.bfloat16)
                out_ref[freq, kind, side * LANES : (side + 1) * LANES] = lax.dot_general(
                    value, right, (((0,), (0,)), ((), ())), preferred_element_type=jnp.float32
                ).astype(jnp.bfloat16)


def on_device(sizes, valence, conduction, val_energy, cond_energy, frequencies, gvec_index, first_band):
    band_count, grow_count, gcol_count = sizes
    devices = band_count * grow_count * gcol_count
    bands = cond_energy.shape[0]
    val_count = val_energy.shape[0]
    freq_count = frequencies.shape[0]
    num_gvec = gvec_index.shape[0]
    tiles = tile_density(valence, conduction, gvec_index)
    num_tiles = tiles.shape[0]
    col_tiles = num_tiles // gcol_count
    gap_value = cond_energy[None, :] - val_energy[:, None]
    counted = jnp.arange(bands, dtype=jnp.int32)[None, :] >= first_band[:, None]
    weight = (
        jnp.where(
            counted[None],
            -4.0 * gap_value[None] / (gap_value[None] ** 2 + frequencies[:, None, None] ** 2),
            0.0,
        )
        / (bands * val_count)
    )
    weight = jnp.transpose(weight, (0, 2, 1))[:, :, None, :, None]
    weight = jnp.broadcast_to(weight, (freq_count, bands, 2, val_count, LANES))
    weight = weight.reshape(freq_count, bands, 2 * val_count, LANES)
    out = pl.pallas_call(
        functools.partial(exchange_kernel, sizes),
        out_shape=jax.ShapeDtypeStruct((freq_count, 2, TILE, num_gvec // gcol_count), jnp.bfloat16),
        in_specs=[pl.BlockSpec(memory_space=pltpu.VMEM)] * 2,
        out_specs=pl.BlockSpec(memory_space=pltpu.VMEM),
        scratch_shapes=[
            pltpu.VMEM((devices,) + tiles.shape[1:], jnp.bfloat16),
            pltpu.VMEM((devices, col_tiles) + tiles.shape[1:], jnp.bfloat16),
            pltpu.SemaphoreType.DMA((2,)),
            pltpu.SemaphoreType.DMA((2,)),
            pltpu.SemaphoreType.DMA,
        ],
        compiler_params=pltpu.CompilerParams(
            collective_id=0, has_side_effects=True, vmem_limit_bytes=48 * 2**20
        ),
    )(tiles, weight)
    out = jnp.transpose(out, (2, 0, 1, 3))
    row_count = num_gvec // (grow_count * band_count)
    if row_count < TILE:
        block = lax.axis_index("grow") * band_count + lax.axis_index("band")
        out = lax.dynamic_slice_in_dim(out, block * row_count % TILE, row_count, 0)
    return out


def solution(mesh):
    sizes = tuple(mesh.shape[name] for name in ("band", "grow", "gcol"))
    return jax.shard_map(
        functools.partial(on_device, sizes),
        mesh=mesh,
        in_specs=(P(), P(("band", "grow", "gcol"), None), P(), P(), P(), P(), P()),
        out_specs=P(("grow", "band"), None, None, "gcol"),
        check_vma=False,
    )
```

profile of v0, /device:TPU:0, one launch (start us, length us, event | category | flops | bytes accessed | tf_op | source)
XLA Modules:
  0.0 43.9 jit_solution(18220354842650159471)
XLA Ops:
  0.0 0.7 %integer_pow.14 = f32[2]{0:T(128)S(1)} multiply(f32[2]{0:T(128)} %param.13, f32[2]{0:T(128)} %param.13) | non-fusion elementwise | flops 2 | bytes 24 | tf_op jit(solution)/shard_map/integer_pow | solution.py:225
  0.7 0.7 %iota_compare_fusion = pred[32,4]{0,1:T(4,128)(4,1)S(1)} fusion(s32[4]{0:T(128)} %param.15), kind=kLoop, calls=%fused_computation.3 | loop fusion | flops 128 | bytes 144 | tf_op jit(solution)/shard_map/ge | solution.py:221
  1.5 0.7 %subtract_multiply_fusion.1 = (f32[32,4]{0,1:T(4,128)S(1)}, f32[32,4]{0,1:T(4,128)S(1)}) fusion(f32[4]{0:T(128)} %param.11, f32[32]{0:T(128)} %param.12), kind=kLoop, calls=%fused_computation.2 | loop fusion | flops 384 | bytes 1168 | tf_op jit(solution)/shard_map/mul | solution.py:225
  2.2 0.1 select_multiply_fusion
  2.3 0.1 copy.11
  2.4 2.2 %reduce = bf16[110592]{0:T(1024)(128)(2,1)S(1)} reduce(bf16[1,110592]{1,0:T(2,128)(2,1)} %param.10, bf16[]{:T(256)} %constant.14), dimensions={0}, to_apply=%param.10.reduce_sub_computation | reduce | bytes 442370 | tf_op args[1]
  4.6 0.3 reshape.95.cond_ref
  4.9 0.1 broadcast_in_dim.34.weight_ref
  5.0 2.0 %reshape.94.val_ref = bf16[192,2304]{1,0:T(8,128)(2,1)S(1)} reshape(bf16[4,110592]{1,0:T(4,128)(2,1)} %param.9) | data formatting | bytes 1769472 | tf_op jit(solution)/shard_map/reshape | solution.py:135
  7.0 0.0 copy-start
  7.0 0.8 %copy-done = bf16[192,128]{1,0:T(8,128)(2,1)S(1)} copy-done((bf16[192,128]{1,0:T(8,128)(2,1)S(1)}, bf16[192,128]{1,0:T(8,128)(2,1)}, u32[]{:S(2)}) %copy-start) | copy-done | bytes 49176
  7.8 0.0 copy-start.1
  7.8 0.7 %copy-done.1 = s32[2048]{0:T(1024)S(1)} copy-done((s32[2048]{0:T(1024)S(1)}, s32[2048]{0:T(1024)}, u32[]{:S(2)}) %copy-start.1) | copy-done | bytes 8216
  8.5 17.1 %shard_map.91.tiles_ref = bf16[8,16,128]{2,1,0:T(8,128)(2,1)S(1)} custom-call(bf16[192,2304]{1,0:T(8,128)(2,1)S(1)} %reshape.94.val_ref, bf16[48,2304]{1,0:T(8,128)(2,1)S(1)} %reshape.95.cond_ref, bf16[10,2304,256]{2,1,0:T(8,128)(2,1)} %constant.11.clone.table_ref, bf16[192,128]{1,0:T(8,128)(2,1)S(1)} %copy-done, s32[8,1,256]{2,1,0:T(1,128)S(1)} %bitcast.4), custom_call_target="tpu_custom_call" | custom-call | tf_op jit(solution)/shard_map/pallas_call | solution.py:117
  25.6 16.2 %shard_map.92 = bf16[2,2,256,512]{3,2,1,0:T(8,128)(2,1)S(1)} custom-call(bf16[8,16,128]{2,1,0:T(8,128)(2,1)S(1)} %shard_map.91.tiles_ref, f32[2,32,8,128]{3,2,1,0:T(8,128)S(1)} %broadcast_in_dim.34.weight_ref), custom_call_target="tpu_custom_call" | custom-call | tf_op jit(solution)/shard_map/pallas_call | solution.py:233
  41.8 2.0 %copy.12 = bf16[256,2,2,512]{3,2,1,0:T(2,128)(2,1)} copy(bf16[256,2,2,512]{3,0,2,1:T(8,128)(2,1)S(1)} %bitcast.3) | data formatting | bytes 2097152 | tf_op jit(solution)/shard_map/transpose | solution.py:249
  (1 shorter events, 0.0 us)
Async XLA Ops:
  7.0 0.8 %copy-start = (bf16[192,128]{1,0:T(8,128)(2,1)S(1)}, bf16[192,128]{1,0:T(8,128)(2,1)}, u32[]{:S(2)}) copy-start(bf16[192,128]{1,0:T(8,128)(2,1)} %constant.12.clone.phase_ref) | copy-start | bytes 147460
  7.8 0.7 %copy-start.1 = (s32[2048]{0:T(1024)S(1)}, s32[2048]{0:T(1024)}, u32[]{:S(2)}) copy-start(s32[2048]{0:T(1024)} %param.14) | copy-start | bytes 24580
where the time goes:
time: 44.4 us; the launch traced here: 43.9 us
  Pallas kernels  33.3 us (75%)
  local copies, waits for them, and re-layouts  5.99 us (13%)
  other arithmetic  4.52 us (10%)
    pallas_call x1, Pallas kernels, tile_density(): pl.pallas_call(density_kernel, grid=(2 * CHUNKS,), out_shape=jax.ShapeDty...  17.1 us
    pallas_call x1, Pallas kernels, on_device(): pl.pallas_call(functools.partial(exchange_kernel, sizes), out_shape=jax.S...  16.2 us
    unnamed x1, other arithmetic  2.24 us
    transpose x1, local copies, waits for them, and re-layouts, on_device(): out = jnp.transpose(out, (2, 0, 1, 3))  2.05 us
    reshape x1, local copies, waits for them, and re-layouts, tile_density(): valence.reshape(rows, PLANE)  1.97 us
    unnamed x4, local copies, waits for them, and re-layouts  1.49 us

commit v1 on v0

v1 whole, which is shorter than its diff:
```python
import functools
import math

import jax
import jax.numpy as jnp
import ml_dtypes
import numpy as np
from jax import lax
from jax.experimental import pallas as pl
from jax.experimental.pallas import tpu as pltpu
from jax.sharding import PartitionSpec as P

GRID = 48
HALF = GRID // 2 + 1
PLANE = GRID * GRID
CHUNK = 256
CHUNKS = -(-GRID * HALF // CHUNK)
TILE = 256
LANES = 128
MESH = pl.DeviceIdType.MESH
TABLE_SCALE = 1.622
TABLE_GAIN = 1.6242055647


def plane_table():
    line = np.arange(GRID)
    k2, k3 = np.meshgrid(line, np.arange(HALF), indexing="ij")
    k2, k3 = k2.reshape(-1), k3.reshape(-1)
    b, e = np.meshgrid(line, line, indexing="ij")
    b, e = b.reshape(-1), e.reshape(-1)
    turn = (b[:, None] * k2[None] + e[:, None] * k3[None]) % GRID
    angle = 2.0 * np.pi * line / GRID
    parts = []
    for values in (np.cos(angle), -np.sin(angle)):
        small = (values * TABLE_SCALE).astype(np.float32).astype(ml_dtypes.bfloat16)
        full = np.zeros((PLANE, CHUNKS * CHUNK), ml_dtypes.bfloat16)
        full[:, : GRID * HALF] = small[turn]
        parts.append(full.reshape(PLANE, CHUNKS, CHUNK).transpose(1, 0, 2))
    return np.concatenate(parts, 0)


def phase_table(val_count):
    line = np.arange(GRID)
    angle = 2.0 * np.pi * (line[:, None] * line[None] % GRID) / GRID
    scale = GRID ** (-1.5) / TABLE_GAIN
    both = np.concatenate([np.cos(angle), np.sin(angle)], 0).astype(np.float64) * scale
    both = np.repeat(both, val_count, 0).astype(np.float32)
    high = both.astype(ml_dtypes.bfloat16)
    low = (both - high.astype(np.float32)).astype(ml_dtypes.bfloat16)
    table = np.zeros((both.shape[0], LANES), ml_dtypes.bfloat16)
    table[:, :GRID] = high
    table[:, LANES // 2 : LANES // 2 + GRID] = low
    return table


def kernel(
    sizes, val_ref, cond_ref, table_ref, phase_ref, index_ref, val_energy, cond_energy, frequencies, first_band,
    out_ref, pair, planes, tiles, from_line, rows_in, cols_in, line_send, line_recv, plane_send, plane_recv,
):
    band_count, grow_count, gcol_count = sizes
    plane_count = band_count * gcol_count
    devices = plane_count * grow_count
    step = pl.program_id(0)
    val_count = val_ref.shape[0]
    rows = val_count * GRID
    num_tiles = tiles.shape[0]
    col_tiles = num_tiles // gcol_count
    freq_count = out_ref.shape[0]
    band, grow, gcol = (lax.axis_index(name) for name in ("band", "grow", "gcol"))
    plane = band * gcol_count + gcol
    barrier = pltpu.get_barrier_semaphore()

    def line_peer(offset):
        return band, lax.rem(grow + offset, grow_count), gcol

    def plane_peer(offset):
        number = lax.rem(plane + offset, plane_count)
        return number // gcol_count, grow, number % gcol_count

    def number_of(place):
        return (place[0] * grow_count + place[1]) * gcol_count + place[2]

    def row_tile(place):
        return (place[1] * band_count + place[0]) * num_tiles // (grow_count * band_count)

    @pl.when(step == 0)
    def _():
        for offset in range(1, grow_count):
            pl.semaphore_signal(barrier, inc=1, device_id=line_peer(offset), device_id_type=MESH)

        @pl.loop(1, plane_count)
        def _(offset):
            pl.semaphore_signal(barrier, inc=1, device_id=plane_peer(offset), device_id_type=MESH)

        group = 16 // val_count

        @pl.loop(0, GRID // group)
        def _(block):
            products = []
            for member in range(group):
                where = pl.ds(pl.multiple_of((block * group + member) * PLANE, LANES), PLANE)
                products.append(
                    val_ref[:, where].astype(jnp.float32) * cond_ref[:, where].astype(jnp.float32)
                )
            product = jnp.concatenate(products, 0)
            high = product.astype(jnp.bfloat16)
            start = pl.multiple_of(block * 16, 16)
            pair[pl.ds(start, 16)] = high
            pair[pl.ds(rows + start, 16)] = (product - high.astype(jnp.float32)).astype(jnp.bfloat16)

    both = jnp.dot(pair[...], table_ref[0], preferred_element_type=jnp.float32)
    total = both[:rows] + both[rows:]
    high = total.astype(jnp.bfloat16)
    planes[step, :rows] = high
    planes[step, rows:] = (total - high.astype(jnp.float32)).astype(jnp.bfloat16)

    @pl.when(step == 2 * CHUNKS - 1)
    def _():
        pl.semaphore_wait(barrier, grow_count - 1 + plane_count - 1)

        @pl.loop(0, num_tiles)
        def _(tile):
            index = index_ref[tile]
            index_float = index.astype(jnp.float32)
            upper = jnp.floor((index_float + 0.5) * (1.0 / GRID))
            k3 = index_float - GRID * upper
            k1 = jnp.floor((upper + 0.5) * (1.0 / GRID))
            k2 = upper - GRID * k1
            mirror = k3 > HALF - 1
            k1 = jnp.where(mirror & (k1 > 0), GRID - k1, k1).astype(jnp.int32)
            k2 = jnp.where(mirror & (k2 > 0), GRID - k2, k2)
            k3 = jnp.where(mirror, GRID - k3, k3)
            sign = jnp.where(mirror, -1.0, 1.0)
            place = (k2 * HALF + k3).astype(jnp.int32)
            real = jnp.zeros((2 * rows, TILE), jnp.float32)
            imag = jnp.zeros((2 * rows, TILE), jnp.float32)
            line = lax.broadcasted_iota(jnp.int32, (CHUNK, TILE), 0)
            for chunk in range(CHUNKS):
                pick = jnp.where(line == place - chunk * CHUNK, 1.0, 0.0).astype(jnp.bfloat16)
                real += jnp.dot(planes[chunk], pick, preferred_element_type=jnp.float32)
                imag += jnp.dot(planes[CHUNKS + chunk], pick, preferred_element_type=jnp.float32)
            real = real[:rows] + real[rows:]
            imag = imag[:rows] + imag[rows:]
            line = line[:LANES]
            pick = jnp.where((line == k1) | (line == k1 + LANES // 2), 1.0, 0.0).astype(jnp.bfloat16)
            phases = jnp.dot(phase_ref[...], pick, preferred_element_type=jnp.float32)
            cos_one, sin_one = phases[:rows], phases[rows:]
            out = []
            for value, flip in (
                (real * cos_one + imag * sin_one, None),
                (imag * cos_one - real * sin_one, sign),
            ):
                value = jnp.sum(value.reshape(rows // 8, 8, TILE), axis=0)
                value = sum(value[n * val_count : (n + 1) * val_count] for n in range(8 // val_count))
                out.append(value if flip is None else value * flip)
            out = jnp.concatenate(out, 0)
            out = jnp.concatenate([out[:, :LANES], out[:, LANES:]], 0)
            tiles[tile] = out.astype(jnp.bfloat16)
            for offset in range(1, grow_count):
                pltpu.make_async_remote_copy(
                    tiles.at[tile], from_line.at[offset - 1, tile], line_send, line_recv.at[offset - 1],
                    device_id=line_peer(offset), device_id_type=MESH,
                ).start()

        def spread(source, origin):
            @pl.loop(1, plane_count)
            def _(offset):
                place = plane_peer(offset)
                pltpu.make_async_remote_copy(
                    source.at[row_tile(place)], rows_in.at[origin], plane_send.at[0], plane_recv.at[0],
                    device_id=place, device_id_type=MESH,
                ).start()
                pltpu.make_async_remote_copy(
                    source.at[pl.ds(place[2] * col_tiles, col_tiles)], cols_in.at[origin],
                    plane_send.at[1], plane_recv.at[1],
                    device_id=place, device_id_type=MESH,
                ).start()

            place = (band, grow, gcol)
            pltpu.make_async_copy(source.at[row_tile(place)], rows_in.at[origin], plane_recv.at[0]).start()
            pltpu.make_async_copy(
                source.at[pl.ds(gcol * col_tiles, col_tiles)], cols_in.at[origin], plane_recv.at[1]
            ).start()

        spread(tiles, number_of((band, grow, gcol)))
        for offset in range(1, grow_count):
            arrived = from_line.at[offset - 1]
            pltpu.make_async_copy(arrived, arrived, line_recv.at[offset - 1]).wait()
            spread(arrived, number_of(line_peer(grow_count - offset)))

        half = 2 * val_count
        depth = devices * half
        row = lax.broadcasted_iota(jnp.int32, (depth, 1), 0)

        def along_rows(values, number):
            lane = lax.broadcasted_iota(jnp.int32, (depth, values.shape[1]), 1)
            return jnp.sum(jnp.where(lane == number, values, 0), axis=1, keepdims=True)

        band_id = row // half
        val_id = row % val_count
        gap = along_rows(cond_energy[...], band_id) - along_rows(val_energy[...], val_id)
        counted = band_id >= along_rows(first_band[...], val_id)
        weights = []
        for freq in range(freq_count):
            denominator = gap * gap + frequencies[:, freq : freq + 1] * frequencies[:, freq : freq + 1]
            weights.append(jnp.where(counted, -4.0 * gap / denominator, 0.0) / (devices * val_count))

        pltpu.make_async_copy(rows_in, rows_in, plane_recv.at[0]).wait()
        pltpu.make_async_copy(cols_in, cols_in, plane_recv.at[1]).wait()

        cols = cols_in[...].astype(jnp.float32)
        right = jnp.concatenate(
            [cols[:, tile, side * half : (side + 1) * half].reshape(depth, LANES)
             for tile in range(col_tiles) for side in range(2)], 1
        ).astype(jnp.bfloat16)
        inward = rows_in[...].astype(jnp.float32)
        for side in range(2):
            part = inward[:, side * half : (side + 1) * half].reshape(depth, LANES)
            for freq in range(freq_count):
                left = part * weights[freq]
                cube = left.reshape(devices, half, LANES)
                swapped = jnp.concatenate([cube[:, val_count:], -cube[:, :val_count]], 1)
                for kind, value in enumerate((left, swapped.reshape(depth, LANES))):
                    out_ref[freq, kind, side * LANES : (side + 1) * LANES] = lax.dot_general(
                        value.astype(jnp.bfloat16), right, (((0,), (0,)), ((), ())),
                        preferred_element_type=jnp.float32,
                    ).astype(jnp.bfloat16)

        pltpu.make_async_copy(from_line, from_line, line_send).wait()
        for held, sem in ((rows_in, 0), (cols_in, 1)):
            sent = held.at[pl.ds(0, (plane_count - 1) * grow_count)]
            pltpu.make_async_copy(sent, sent, plane_send.at[sem]).wait()


def on_device(sizes, valence, conduction, val_energy, cond_energy, frequencies, gvec_index, first_band):
    band_count, grow_count, gcol_count = sizes
    devices = band_count * grow_count * gcol_count
    val_count = val_energy.shape[0]
    freq_count = frequencies.shape[0]
    num_gvec = gvec_index.shape[0]
    rows = val_count * GRID
    num_tiles = num_gvec // TILE
    col_tiles = num_tiles // gcol_count
    tile_shape = (4 * val_count, LANES)
    operands = (
        valence,
        conduction,
        jnp.asarray(plane_table()),
        jnp.asarray(phase_table(val_count)),
        gvec_index.reshape(num_tiles, 1, TILE),
        val_energy[None],
        cond_energy[None],
        frequencies[None],
        first_band[None],
    )
    specs = [pl.BlockSpec(a.shape, lambda n, rank=a.ndim: (0,) * rank) for a in operands]
    specs[2] = pl.BlockSpec((1, PLANE, CHUNK), lambda n: (n, 0, 0))
    out_shape = (freq_count, 2, TILE, num_gvec // gcol_count)
    out = pl.pallas_call(
        functools.partial(kernel, sizes),
        grid=(2 * CHUNKS,),
        out_shape=jax.ShapeDtypeStruct(out_shape, jnp.bfloat16),
        in_specs=specs,
        out_specs=pl.BlockSpec(out_shape, lambda n: (0, 0, 0, 0)),
        scratch_shapes=[
            pltpu.VMEM((2 * rows, PLANE), jnp.bfloat16),
            pltpu.VMEM((2 * CHUNKS, 2 * rows, CHUNK), jnp.bfloat16),
            pltpu.VMEM((num_tiles,) + tile_shape, jnp.bfloat16),
            pltpu.VMEM((grow_count - 1, num_tiles) + tile_shape, jnp.bfloat16),
            pltpu.VMEM((devices,) + tile_shape, jnp.bfloat16),
            pltpu.VMEM((devices, col_tiles) + tile_shape, jnp.bfloat16),
            pltpu.SemaphoreType.DMA,
            pltpu.SemaphoreType.DMA((grow_count - 1,)),
            pltpu.SemaphoreType.DMA((2,)),
            pltpu.SemaphoreType.DMA((2,)),
        ],
        compiler_params=pltpu.CompilerParams(
            collective_id=0, has_side_effects=True, vmem_limit_bytes=48 * 2**20
        ),
    )(*operands)
    out = jnp.transpose(out, (2, 0, 1, 3))
    row_count = num_gvec // (grow_count * band_count)
    if row_count < TILE:
        block = lax.axis_index("grow") * band_count + lax.axis_index("band")
        out = lax.dynamic_slice_in_dim(out, block * row_count % TILE, row_count, 0)
    return out


def solution(mesh):
    sizes = tuple(mesh.shape[name] for name in ("band", "grow", "gcol"))
    return jax.shard_map(
        functools.partial(on_device, sizes),
        mesh=mesh,
        in_specs=(P(), P(("band", "grow", "gcol"), None), P(), P(), P(), P(), P()),
        out_specs=P(("grow", "band"), None, None, "gcol"),
        check_vma=False,
    )
```

time: 44.4 us -> 39.1 us (0.88)
  other arithmetic: 4.52 us -> 0 us
  Pallas kernels: 33.3 us -> 30.2 us
  local copies, waits for them, and re-layouts: 5.99 us -> 8.44 us
    unnamed x4 -> x16, local copies, waits for them, and re-layouts: 1.49 us -> 6.39 us
    pallas_call x2 -> x1, Pallas kernels: 33.3 us -> 30.2 us  [on_device(): pl.pallas_call(functools.partial(kernel, sizes), grid=(2 * CHUNKS,), out_...]
    unnamed x1 -> x0, other arithmetic: 2.24 us -> none
    reshape x2 -> x0, local copies, waits for them, and re-layouts: 2.24 us -> none  [the longest x1 1.97 us: tile_density(): valence.reshape(rows, PLANE)]
    mul x1 -> x0, other arithmetic: 0.74 us -> none  [on_device(): -4.0 * gap_value[None]]
    integer_pow x1 -> x0, other arithmetic: 0.73 us -> none  [on_device(): frequencies[:, None, None] ** 2]
    ge x1 -> x0, other arithmetic: 0.73 us -> none  [on_device(): counted = jnp.arange(bands, dtype=jnp.int32)[None, :] >= first_band[:, None]]
where the time goes in v1:
time: 39.1 us; the launch traced here: 38.6 us
  Pallas kernels  30.2 us (77%)
  local copies, waits for them, and re-layouts  8.44 us (22%)
    pallas_call x1, Pallas kernels, on_device(): pl.pallas_call(functools.partial(kernel, sizes), grid=(2 * CHUNKS,), out_...  30.2 us
    unnamed x16, local copies, waits for them, and re-layouts  6.39 us
    transpose x1, local copies, waits for them, and re-layouts, on_device(): out = jnp.transpose(out, (2, 0, 1, 3))  2.05 us

profile of v1, /device:TPU:0, one launch (start us, length us, event | category | flops | bytes accessed | tf_op | source)
XLA Modules:
  0.0 38.6 jit_solution(5255918702915752689)
XLA Ops:
  0.0 0.0 copy-start
  0.0 1.2 %copy-done = bf16[4,110592]{1,0:T(4,128)(2,1)S(1)} copy-done((bf16[4,110592]{1,0:T(4,128)(2,1)S(1)}, bf16[4,110592]{1,0:T(4,128)(2,1)}, u32[]{:S(2)}) %copy-start) | copy-done | bytes 884760
  1.2 0.0 copy-start.1
  1.2 1.0 %copy-done.1 = bf16[1,110592]{1,0:T(2,128)(2,1)S(1)} copy-done((bf16[1,110592]{1,0:T(2,128)(2,1)S(1)}, bf16[1,110592]{1,0:T(2,128)(2,1)}, u32[]{:S(2)}) %copy-start.1) | copy-done | bytes 221208
  2.2 0.0 copy-start.2
  2.2 0.9 %copy-done.2 = bf16[384,128]{1,0:T(8,128)(2,1)S(1)} copy-done((bf16[384,128]{1,0:T(8,128)(2,1)S(1)}, bf16[384,128]{1,0:T(8,128)(2,1)}, u32[]{:S(2)}) %copy-start.2) | copy-done | bytes 98328
  3.1 0.0 copy-start.3
  3.1 0.7 %copy-done.3 = s32[2048]{0:T(1024)S(1)} copy-done((s32[2048]{0:T(1024)S(1)}, s32[2048]{0:T(1024)}, u32[]{:S(2)}) %copy-start.3) | copy-done | bytes 8216
  3.8 0.0 copy-start.4
  3.8 0.7 %copy-done.4 = f32[4]{0:T(128)S(1)} copy-done((f32[4]{0:T(128)S(1)}, f32[4]{0:T(128)}, u32[]{:S(2)}) %copy-start.4) | copy-done | bytes 40
  4.4 0.0 copy-start.5
  4.4 0.7 %copy-done.5 = f32[32]{0:T(128)S(1)} copy-done((f32[32]{0:T(128)S(1)}, f32[32]{0:T(128)}, u32[]{:S(2)}) %copy-start.5) | copy-done | bytes 152
  5.1 0.0 copy-start.6
  5.1 0.7 %copy-done.6 = f32[2]{0:T(128)S(1)} copy-done((f32[2]{0:T(128)S(1)}, f32[2]{0:T(128)}, u32[]{:S(2)}) %copy-start.6) | copy-done | bytes 32
  5.7 0.0 copy-start.7
  5.7 0.7 %copy-done.7 = s32[4]{0:T(128)S(1)} copy-done((s32[4]{0:T(128)S(1)}, s32[4]{0:T(128)}, u32[]{:S(2)}) %copy-start.7) | copy-done | bytes 40
  6.4 30.2 %shard_map.91 = bf16[2,2,256,512]{3,2,1,0:T(8,128)(2,1)S(1)} custom-call(bf16[4,110592]{1,0:T(4,128)(2,1)S(1)} %copy-done, bf16[1,110592]{1,0:T(2,128)(2,1)S(1)} %copy-done.1, bf16[10,2304,256]{2,1,0:T(8,128)(2,1)} %constant.4.clone.table_ref, bf16[384,128]{1,0:T(8,128)(2,1)S(1)} %copy-done.2, s32[8,1,256]{2,1,0:T(1,128)S(1)} %bitcast.7, ...), custom_call_target="tpu_custom_call" | custom-call | tf_op jit(solution)/shard_map/pallas_call | solution.py:259
  36.6 2.0 %copy.10 = bf16[256,2,2,512]{3,2,1,0:T(2,128)(2,1)} copy(bf16[256,2,2,512]{3,0,2,1:T(8,128)(2,1)S(1)} %bitcast.6) | data formatting | bytes 2097152 | tf_op jit(solution)/shard_map/transpose | solution.py:281
Async XLA Ops:
  0.0 1.2 %copy-start = (bf16[4,110592]{1,0:T(4,128)(2,1)S(1)}, bf16[4,110592]{1,0:T(4,128)(2,1)}, u32[]{:S(2)}) copy-start(bf16[4,110592]{1,0:T(4,128)(2,1)} %val_ref.1) | copy-start | bytes 2654212
  1.2 1.0 %copy-start.1 = (bf16[1,110592]{1,0:T(2,128)(2,1)S(1)}, bf16[1,110592]{1,0:T(2,128)(2,1)}, u32[]{:S(2)}) copy-start(bf16[1,110592]{1,0:T(2,128)(2,1)} %cond_ref.1) | copy-start | bytes 663556
  2.2 0.9 %copy-start.2 = (bf16[384,128]{1,0:T(8,128)(2,1)S(1)}, bf16[384,128]{1,0:T(8,128)(2,1)}, u32[]{:S(2)}) copy-start(bf16[384,128]{1,0:T(8,128)(2,1)} %constant.5.clone.phase_ref) | copy-start | bytes 294916
  3.1 0.7 %copy-start.3 = (s32[2048]{0:T(1024)S(1)}, s32[2048]{0:T(1024)}, u32[]{:S(2)}) copy-start(s32[2048]{0:T(1024)} %param.14) | copy-start | bytes 24580
  3.8 0.7 %copy-start.4 = (f32[4]{0:T(128)S(1)}, f32[4]{0:T(128)}, u32[]{:S(2)}) copy-start(f32[4]{0:T(128)} %param.11) | copy-start | bytes 52
  4.4 0.7 %copy-start.5 = (f32[32]{0:T(128)S(1)}, f32[32]{0:T(128)}, u32[]{:S(2)}) copy-start(f32[32]{0:T(128)} %param.12) | copy-start | bytes 388
  5.1 0.7 %copy-start.6 = (f32[2]{0:T(128)S(1)}, f32[2]{0:T(128)}, u32[]{:S(2)}) copy-start(f32[2]{0:T(128)} %param.13) | copy-start | bytes 28
  5.7 0.7 %copy-start.7 = (s32[4]{0:T(128)S(1)}, s32[4]{0:T(128)}, u32[]{:S(2)}) copy-start(s32[4]{0:T(128)} %param.15) | copy-start | bytes 52

commit v2 on v1

--- a/solution.py
+++ b/solution.py
@@ -54,28 +54,49 @@
 
 
 def kernel(
-    sizes, val_ref, cond_ref, table_ref, phase_ref, index_ref, val_energy, cond_energy, frequencies, first_band,
-    out_ref, pair, planes, tiles, from_line, rows_in, cols_in, line_send, line_recv, plane_send, plane_recv,
+    sizes, val_hbm, cond_hbm, table_hbm, phase_ref, index_ref, val_energy, cond_energy, frequencies, first_band,
+    out_ref, val_ref, cond_ref, table_ref, pair, planes, tiles, from_line, rows_in, cols_in,
+    load, table_load, line_send, line_recv, plane_send, plane_recv,
 ):
     band_count, grow_count, gcol_count = sizes
     plane_count = band_count * gcol_count
     devices = plane_count * grow_count
-    step = pl.program_id(0)
     val_count = val_ref.shape[0]
     rows = val_count * GRID
     num_tiles = tiles.shape[0]
     col_tiles = num_tiles // gcol_count
     freq_count = out_ref.shape[0]
     band, grow, gcol = (lax.axis_index(name) for name in ("band", "grow", "gcol"))
-    plane = band * gcol_count + gcol
     barrier = pltpu.get_barrier_semaphore()
 
+    loads = [pltpu.make_async_copy(val_hbm, val_ref, load.at[0]), pltpu.make_async_copy(cond_hbm, cond_ref, load.at[1])]
+    table_loads = [
+        pltpu.make_async_copy(table_hbm.at[n], table_ref.at[n], table_load.at[n]) for n in range(2 * CHUNKS)
+    ]
+    for copy in loads + table_loads:
+        copy.start()
+
+    def turned(place, offset, count):
+        place = place + offset
+        return jnp.where(place >= count, place - count, place)
+
     def line_peer(offset):
-        return band, lax.rem(grow + offset, grow_count), gcol
-
-    def plane_peer(offset):
-        number = lax.rem(plane + offset, plane_count)
-        return number // gcol_count, grow, number % gcol_count
+        return band, turned(grow, offset, grow_count), gcol
+
+    gcols = [turned(gcol, offset, gcol_count) for offset in range(gcol_count)]
+
+    def each_plane_peer(body):
+        def one_band(offset, first):
+            to_band = turned(band, offset, band_count) if not first else band
+            for gcol_offset in range(1 if first else 0, gcol_count):
+                body((to_band, grow, gcols[gcol_offset]))
+
+        one_band(0, True)
+        if band_count <= 2:
+            for offset in range(1, band_count):
+                one_band(offset, False)
+        else:
+            pl.loop(1, band_count)(lambda offset: one_band(offset, False))
 
     def number_of(place):
         return (place[0] * grow_count + place[1]) * gcol_count + place[2]
@@ -83,39 +104,40 @@
     def row_tile(place):
         return (place[1] * band_count + place[0]) * num_tiles // (grow_count * band_count)
 
-    @pl.when(step == 0)
-    def _():
-        for offset in range(1, grow_count):
-            pl.semaphore_signal(barrier, inc=1, device_id=line_peer(offset), device_id_type=MESH)
-
-        @pl.loop(1, plane_count)
-        def _(offset):
-            pl.semaphore_signal(barrier, inc=1, device_id=plane_peer(offset), device_id_type=MESH)
-
-        group = 16 // val_count
-
-        @pl.loop(0, GRID // group)
-        def _(block):
-            products = []
-            for member in range(group):
-                where = pl.ds(pl.multiple_of((block * group + member) * PLANE, LANES), PLANE)
-                products.append(
-                    val_ref[:, where].astype(jnp.float32) * cond_ref[:, where].astype(jnp.float32)
-                )
-            product = jnp.concatenate(products, 0)
-            high = product.astype(jnp.bfloat16)
-            start = pl.multiple_of(block * 16, 16)
-            pair[pl.ds(start, 16)] = high
-            pair[pl.ds(rows + start, 16)] = (product - high.astype(jnp.float32)).astype(jnp.bfloat16)
-
-    both = jnp.dot(pair[...], table_ref[0], preferred_element_type=jnp.float32)
-    total = both[:rows] + both[rows:]
-    high = total.astype(jnp.bfloat16)
-    planes[step, :rows] = high
-    planes[step, rows:] = (total - high.astype(jnp.float32)).astype(jnp.bfloat16)
-
-    @pl.when(step == 2 * CHUNKS - 1)
-    def _():
+    def greet(place):
+        pl.semaphore_signal(barrier, inc=1, device_id=place, device_id_type=MESH)
+
+    for offset in range(1, grow_count):
+        greet(line_peer(offset))
+    each_plane_peer(greet)
+
+    for copy in loads:
+        copy.wait()
+    group = 16 // val_count
+
+    @pl.loop(0, GRID // group)
+    def _(block):
+        products = []
+        for member in range(group):
+            where = pl.ds(pl.multiple_of((block * group + member) * PLANE, LANES), PLANE)
+            products.append(val_ref[:, where].astype(jnp.float32) * cond_ref[:, where].astype(jnp.float32))
+        product = jnp.concatenate(products, 0)
+        high = product.astype(jnp.bfloat16)
+        start = pl.multiple_of(block * 16, 16)
+        pair[pl.ds(start, 16)] = high
+        pair[pl.ds(rows + start, 16)] = (product - high.astype(jnp.float32)).astype(jnp.bfloat16)
+
+    for step in range(2 * CHUNKS):
+        table_loads[step].wait()
+        both = jnp.dot(pair[...], table_ref[step], preferred_element_type=jnp.float32)
+        total = both[:rows] + both[rows:]
+        high = total.astype(jnp.bfloat16)
+        start = step // CHUNKS * 2 * rows
+        where = pl.ds(step % CHUNKS * CHUNK, CHUNK)
+        planes[start : start + rows, where] = high
+        planes[start + rows : start + 2 * rows, where] = (total - high.astype(jnp.float32)).astype(jnp.bfloat16)
+
+    if True:
         pl.semaphore_wait(barrier, grow_count - 1 + plane_count - 1)
 
         @pl.loop(0, num_tiles)
@@ -132,15 +154,11 @@
             k3 = jnp.where(mirror, GRID - k3, k3)
             sign = jnp.where(mirror, -1.0, 1.0)
             place = (k2 * HALF + k3).astype(jnp.int32)
-            real = jnp.zeros((2 * rows, TILE), jnp.float32)
-            imag = jnp.zeros((2 * rows, TILE), jnp.float32)
-            line = lax.broadcasted_iota(jnp.int32, (CHUNK, TILE), 0)
-            for chunk in range(CHUNKS):
-                pick = jnp.where(line == place - chunk * CHUNK, 1.0, 0.0).astype(jnp.bfloat16)
-                real += jnp.dot(planes[chunk], pick, preferred_element_type=jnp.float32)
-                imag += jnp.dot(planes[CHUNKS + chunk], pick, preferred_element_type=jnp.float32)
-            real = real[:rows] + real[rows:]
-            imag = imag[:rows] + imag[rows:]
+            line = lax.broadcasted_iota(jnp.int32, (CHUNKS * CHUNK, TILE), 0)
+            pick = jnp.where(line == place, 1.0, 0.0).astype(jnp.bfloat16)
+            picked = jnp.dot(planes[...], pick, preferred_element_type=jnp.float32)
+            real = picked[:rows] + picked[rows : 2 * rows]
+            imag = picked[2 * rows : 3 * rows] + picked[3 * rows :]
             line = line[:LANES]
             pick = jnp.where((line == k1) | (line == k1 + LANES // 2), 1.0, 0.0).astype(jnp.bfloat16)
             phases = jnp.dot(phase_ref[...], pick, preferred_element_type=jnp.float32)
@@ -163,9 +181,7 @@
                 ).start()
 
         def spread(source, origin):
-            @pl.loop(1, plane_count)
-            def _(offset):
-                place = plane_peer(offset)
+            def send(place):
                 pltpu.make_async_remote_copy(
                     source.at[row_tile(place)], rows_in.at[origin], plane_send.at[0], plane_recv.at[0],
                     device_id=place, device_id_type=MESH,
@@ -176,6 +192,7 @@
                     device_id=place, device_id_type=MESH,
                 ).start()
 
+            each_plane_peer(send)
             place = (band, grow, gcol)
             pltpu.make_async_copy(source.at[row_tile(place)], rows_in.at[origin], plane_recv.at[0]).start()
             pltpu.make_async_copy(
@@ -253,29 +270,32 @@
         frequencies[None],
         first_band[None],
     )
-    specs = [pl.BlockSpec(a.shape, lambda n, rank=a.ndim: (0,) * rank) for a in operands]
-    specs[2] = pl.BlockSpec((1, PLANE, CHUNK), lambda n: (n, 0, 0))
+    specs = [pl.BlockSpec(memory_space=pl.ANY)] * 3 + [pl.BlockSpec(memory_space=pltpu.VMEM)] * 6
     out_shape = (freq_count, 2, TILE, num_gvec // gcol_count)
     out = pl.pallas_call(
         functools.partial(kernel, sizes),
-        grid=(2 * CHUNKS,),
         out_shape=jax.ShapeDtypeStruct(out_shape, jnp.bfloat16),
         in_specs=specs,
-        out_specs=pl.BlockSpec(out_shape, lambda n: (0, 0, 0, 0)),
+        out_specs=pl.BlockSpec(memory_space=pltpu.VMEM),
         scratch_shapes=[
+            pltpu.VMEM(valence.shape, jnp.bfloat16),
+            pltpu.VMEM(conduction.shape, jnp.bfloat16),
+            pltpu.VMEM((2 * CHUNKS, PLANE, CHUNK), jnp.bfloat16),
             pltpu.VMEM((2 * rows, PLANE), jnp.bfloat16),
-            pltpu.VMEM((2 * CHUNKS, 2 * rows, CHUNK), jnp.bfloat16),
+            pltpu.VMEM((4 * rows, CHUNKS * CHUNK), jnp.bfloat16),
             pltpu.VMEM((num_tiles,) + tile_shape, jnp.bfloat16),
             pltpu.VMEM((grow_count - 1, num_tiles) + tile_shape, jnp.bfloat16),
             pltpu.VMEM((devices,) + tile_shape, jnp.bfloat16),
             pltpu.VMEM((devices, col_tiles) + tile_shape, jnp.bfloat16),
+            pltpu.SemaphoreType.DMA((2,)),
+            pltpu.SemaphoreType.DMA((2 * CHUNKS,)),
             pltpu.SemaphoreType.DMA,
             pltpu.SemaphoreType.DMA((grow_count - 1,)),
             pltpu.SemaphoreType.DMA((2,)),
             pltpu.SemaphoreType.DMA((2,)),
         ],
         compiler_params=pltpu.CompilerParams(
-            collective_id=0, has_side_effects=True, vmem_limit_bytes=48 * 2**20
+            collective_id=0, has_side_effects=True, vmem_limit_bytes=63 * 2**20
         ),
     )(*operands)
     out = jnp.transpose(out, (2, 0, 1, 3))

time: 39.1 us -> 40.5 us (1.036)
  Pallas kernels: 30.2 us -> 37.1 us
  local copies, waits for them, and re-layouts: 8.44 us -> 3.27 us
    pallas_call x1, Pallas kernels: 30.2 us -> 37.1 us  [on_device(): pl.pallas_call(functools.partial(kernel, sizes), out_shape=jax.ShapeDtype...]
    unnamed x16 -> x0, local copies, waits for them, and re-layouts: 6.39 us -> none
    transpose x1, local copies, waits for them, and re-layouts: 2.05 us -> 3.27 us  [on_device(): out = jnp.transpose(out, (2, 0, 1, 3))]
where the time goes in v2:
time: 40.5 us; the launch traced here: 40.4 us
  Pallas kernels  37.1 us (92%)
  local copies, waits for them, and re-layouts  3.27 us (8%)
    pallas_call x1, Pallas kernels, on_device(): pl.pallas_call(functools.partial(kernel, sizes), out_shape=jax.ShapeDtype...  37.1 us
    transpose x1, local copies, waits for them, and re-layouts, on_device(): out = jnp.transpose(out, (2, 0, 1, 3))  3.27 us

profile of v2, /device:TPU:0, one launch (start us, length us, event | category | flops | bytes accessed | tf_op | source)
XLA Modules:
  0.0 40.4 jit_solution(14013538879037477625)
XLA Ops:
  0.0 37.1 %shard_map.91 = bf16[2,2,256,512]{3,2,1,0:T(8,128)(2,1)} custom-call(bf16[4,110592]{1,0:T(4,128)(2,1)} %val_hbm.1, bf16[1,110592]{1,0:T(2,128)(2,1)} %cond_hbm.1, bf16[10,2304,256]{2,1,0:T(8,128)(2,1)} %constant.4.clone.table_hbm, bf16[384,128]{1,0:T(8,128)(2,1)} %constant.5.clone.phase_ref, s32[8,1,256]{2,1,0:T(1,128)} %bitcast.7, f32[1,4]{1,0:T(1,128)} %bitcast.8, ...), custom_call_target="tpu_custom_call" | custom-call | tf_op jit(solution)/shard_map/pallas_call | solution.py:275
  37.1 3.3 %copy.10 = bf16[256,2,2,512]{3,2,1,0:T(2,128)(2,1)} copy(bf16[256,2,2,512]{3,0,2,1:T(8,128)(2,1)} %bitcast.6) | data formatting | bytes 2097152 | tf_op jit(solution)/shard_map/transpose | solution.py:301

commit v3 on v2

v3 whole, which is shorter than its diff:
```python
import functools
import math

import jax
import jax.numpy as jnp
import ml_dtypes
import numpy as np
from jax import lax
from jax.experimental import pallas as pl
from jax.experimental.pallas import tpu as pltpu
from jax.sharding import PartitionSpec as P

GRID = 48
HALF = GRID // 2 + 1
PLANE = GRID * GRID
CHUNK = 256
CHUNKS = -(-GRID * HALF // CHUNK)
TILE = 256
LANES = 128
MESH = pl.DeviceIdType.MESH
TABLE_SCALE = 1.622
TABLE_GAIN = 1.6242055647


def plane_table():
    line = np.arange(GRID)
    k2, k3 = np.meshgrid(line, np.arange(HALF), indexing="ij")
    k2, k3 = k2.reshape(-1), k3.reshape(-1)
    b, e = np.meshgrid(line, line, indexing="ij")
    b, e = b.reshape(-1), e.reshape(-1)
    turn = (b[:, None] * k2[None] + e[:, None] * k3[None]) % GRID
    angle = 2.0 * np.pi * line / GRID
    parts = []
    for values in (np.cos(angle), -np.sin(angle)):
        small = (values * TABLE_SCALE).astype(np.float32).astype(ml_dtypes.bfloat16)
        full = np.zeros((PLANE, CHUNKS * CHUNK), ml_dtypes.bfloat16)
        full[:, : GRID * HALF] = small[turn]
        parts.append(full.reshape(PLANE, CHUNKS, CHUNK).transpose(1, 0, 2))
    return np.concatenate(parts, 0)


def phase_table(val_count):
    line = np.arange(GRID)
    angle = 2.0 * np.pi * (line[:, None] * line[None] % GRID) / GRID
    scale = GRID ** (-1.5) / TABLE_GAIN
    both = np.concatenate([np.cos(angle), np.sin(angle)], 0).astype(np.float64) * scale
    both = np.repeat(both, val_count, 0).astype(np.float32)
    high = both.astype(ml_dtypes.bfloat16)
    low = (both - high.astype(np.float32)).astype(ml_dtypes.bfloat16)
    table = np.zeros((both.shape[0], LANES), ml_dtypes.bfloat16)
    table[:, :GRID] = high
    table[:, LANES // 2 : LANES // 2 + GRID] = low
    return table


def kernel(
    sizes, val_hbm, cond_hbm, table_hbm, phase_hbm, index_hbm, val_energy_hbm, cond_energy_hbm, frequencies_hbm,
    first_band_hbm, out_ref, val_ref, cond_ref, table_ref, phase_ref, index_ref, val_energy, cond_energy,
    frequencies, first_band, pair, planes, tiles, from_line, rows_in, cols_in,
    load, table_load, line_send, line_recv, plane_send, plane_recv,
):
    band_count, grow_count, gcol_count = sizes
    plane_count = band_count * gcol_count
    devices = plane_count * grow_count
    val_count = val_ref.shape[0]
    rows = val_count * GRID
    num_tiles = tiles.shape[0]
    col_tiles = num_tiles // gcol_count
    freq_count = out_ref.shape[0]
    band, grow, gcol = (lax.axis_index(name) for name in ("band", "grow", "gcol"))
    barrier = pltpu.get_barrier_semaphore()

    loads = [pltpu.make_async_copy(val_hbm, val_ref, load.at[0]), pltpu.make_async_copy(cond_hbm, cond_ref, load.at[1])]
    table_loads = [
        pltpu.make_async_copy(table_hbm.at[n], table_ref.at[n], table_load.at[n]) for n in range(2 * CHUNKS)
    ]
    small_loads = [
        pltpu.make_async_copy(source, target, load.at[2 + n])
        for n, (source, target) in enumerate((
            (phase_hbm, phase_ref), (index_hbm, index_ref), (val_energy_hbm, val_energy),
            (cond_energy_hbm, cond_energy), (frequencies_hbm, frequencies), (first_band_hbm, first_band),
        ))
    ]
    for copy in loads + small_loads:
        copy.start()

    def turned(place, offset, count):
        place = place + offset
        return jnp.where(place >= count, place - count, place)

    def line_peer(offset):
        return band, turned(grow, offset, grow_count), gcol

    gcols = [turned(gcol, offset, gcol_count) for offset in range(gcol_count)]

    def each_plane_peer(body):
        def one_band(offset, first):
            to_band = turned(band, offset, band_count) if not first else band
            for gcol_offset in range(1 if first else 0, gcol_count):
                body((to_band, grow, gcols[gcol_offset]))

        one_band(0, True)
        if band_count <= 2:
            for offset in range(1, band_count):
                one_band(offset, False)
        else:
            pl.loop(1, band_count)(lambda offset: one_band(offset, False))

    def number_of(place):
        return (place[0] * grow_count + place[1]) * gcol_count + place[2]

    def row_tile(place):
        return (place[1] * band_count + place[0]) * num_tiles // (grow_count * band_count)

    def greet(place):
        pl.semaphore_signal(barrier, inc=1, device_id=place, device_id_type=MESH)

    for offset in range(1, grow_count):
        greet(line_peer(offset))
    each_plane_peer(greet)

    for copy in loads:
        copy.wait()
    for copy in table_loads:
        copy.start()
    group = 16 // val_count

    @pl.loop(0, GRID // group)
    def _(block):
        products = []
        for member in range(group):
            where = pl.ds(pl.multiple_of((block * group + member) * PLANE, LANES), PLANE)
            products.append(val_ref[:, where].astype(jnp.float32) * cond_ref[:, where].astype(jnp.float32))
        product = jnp.concatenate(products, 0)
        high = product.astype(jnp.bfloat16)
        start = pl.multiple_of(block * 16, 16)
        pair[pl.ds(start, 16)] = high
        pair[pl.ds(rows + start, 16)] = (product - high.astype(jnp.float32)).astype(jnp.bfloat16)

    for step in range(2 * CHUNKS):
        table_loads[step].wait()
        both = jnp.dot(pair[...], table_ref[step], preferred_element_type=jnp.float32)
        total = both[:rows] + both[rows:]
        high = total.astype(jnp.bfloat16)
        start = step // CHUNKS * 2 * rows
        where = pl.ds(step % CHUNKS * CHUNK, CHUNK)
        planes[start : start + rows, where] = high
        planes[start + rows : start + 2 * rows, where] = (total - high.astype(jnp.float32)).astype(jnp.bfloat16)

    for copy in small_loads:
        copy.wait()
    pl.semaphore_wait(barrier, grow_count - 1 + plane_count - 1)

    @pl.loop(0, num_tiles)
    def _(tile):
        index = index_ref[tile]
        index_float = index.astype(jnp.float32)
        upper = jnp.floor((index_float + 0.5) * (1.0 / GRID))
        k3 = index_float - GRID * upper
        k1 = jnp.floor((upper + 0.5) * (1.0 / GRID))
        k2 = upper - GRID * k1
        mirror = k3 > HALF - 1
        k1 = jnp.where(mirror & (k1 > 0), GRID - k1, k1).astype(jnp.int32)
        k2 = jnp.where(mirror & (k2 > 0), GRID - k2, k2)
        k3 = jnp.where(mirror, GRID - k3, k3)
        sign = jnp.where(mirror, -1.0, 1.0)
        place = (k2 * HALF + k3).astype(jnp.int32)
        line = lax.broadcasted_iota(jnp.int32, (CHUNKS * CHUNK, TILE), 0)
        pick = jnp.where(line == place, 1.0, 0.0).astype(jnp.bfloat16)
        picked = jnp.dot(planes[...], pick, preferred_element_type=jnp.float32)
        real = picked[:rows] + picked[rows : 2 * rows]
        imag = picked[2 * rows : 3 * rows] + picked[3 * rows :]
        line = line[:LANES]
        pick = jnp.where((line == k1) | (line == k1 + LANES // 2), 1.0, 0.0).astype(jnp.bfloat16)
        phases = jnp.dot(phase_ref[...], pick, preferred_element_type=jnp.float32)
        cos_one, sin_one = phases[:rows], phases[rows:]
        out = []
        for value, flip in (
            (real * cos_one + imag * sin_one, None),
            (imag * cos_one - real * sin_one, sign),
        ):
            value = jnp.sum(value.reshape(rows // 8, 8, TILE), axis=0)
            value = sum(value[n * val_count : (n + 1) * val_count] for n in range(8 // val_count))
            out.append(value if flip is None else value * flip)
        out = jnp.concatenate(out, 0)
        out = jnp.concatenate([out[:, :LANES], out[:, LANES:]], 0)
        tiles[tile] = out.astype(jnp.bfloat16)
        for offset in range(1, grow_count):
            pltpu.make_async_remote_copy(
                tiles.at[tile], from_line.at[offset - 1, tile], line_send, line_recv.at[offset - 1],
                device_id=line_peer(offset), device_id_type=MESH,
            ).start()

    def spread(source, origin):
        def send(place):
            pltpu.make_async_remote_copy(
                source.at[row_tile(place)], rows_in.at[origin], plane_send.at[0], plane_recv.at[0],
                device_id=place, device_id_type=MESH,
            ).start()
            pltpu.make_async_remote_copy(
                source.at[pl.ds(place[2] * col_tiles, col_tiles)], cols_in.at[origin],
                plane_send.at[1], plane_recv.at[1],
                device_id=place, device_id_type=MESH,
            ).start()

        each_plane_peer(send)
        place = (band, grow, gcol)
        pltpu.make_async_copy(source.at[row_tile(place)], rows_in.at[origin], plane_recv.at[0]).start()
        pltpu.make_async_copy(
            source.at[pl.ds(gcol * col_tiles, col_tiles)], cols_in.at[origin], plane_recv.at[1]
        ).start()

    spread(tiles, number_of((band, grow, gcol)))
    for offset in range(1, grow_count):
        arrived = from_line.at[offset - 1]
        pltpu.make_async_copy(arrived, arrived, line_recv.at[offset - 1]).wait()
        spread(arrived, number_of(line_peer(grow_count - offset)))

    half = 2 * val_count
    depth = devices * half
    row = lax.broadcasted_iota(jnp.int32, (depth, 1), 0)

    def along_rows(values, number):
        lane = lax.broadcasted_iota(jnp.int32, (depth, values.shape[1]), 1)
        return jnp.sum(jnp.where(lane == number, values, 0), axis=1, keepdims=True)

    band_id = row // half
    val_id = row % val_count
    gap = along_rows(cond_energy[...], band_id) - along_rows(val_energy[...], val_id)
    counted = band_id >= along_rows(first_band[...], val_id)
    weights = []
    for freq in range(freq_count):
        denominator = gap * gap + frequencies[:, freq : freq + 1] * frequencies[:, freq : freq + 1]
        weights.append(jnp.where(counted, -4.0 * gap / denominator, 0.0) / (devices * val_count))

    pltpu.make_async_copy(rows_in, rows_in, plane_recv.at[0]).wait()
    pltpu.make_async_copy(cols_in, cols_in, plane_recv.at[1]).wait()

    cols = cols_in[...].astype(jnp.float32)
    right = jnp.concatenate(
        [cols[:, tile, side * half : (side + 1) * half].reshape(depth, LANES)
         for tile in range(col_tiles) for side in range(2)], 1
    ).astype(jnp.bfloat16)
    inward = rows_in[...].astype(jnp.float32)
    for side in range(2):
        part = inward[:, side * half : (side + 1) * half].reshape(depth, LANES)
        for freq in range(freq_count):
            left = part * weights[freq]
            cube = left.reshape(devices, half, LANES)
            swapped = jnp.concatenate([cube[:, val_count:], -cube[:, :val_count]], 1)
            for kind, value in enumerate((left, swapped.reshape(depth, LANES))):
                out_ref[freq, kind, side * LANES : (side + 1) * LANES] = lax.dot_general(
                    value.astype(jnp.bfloat16), right, (((0,), (0,)), ((), ())),
                    preferred_element_type=jnp.float32,
                ).astype(jnp.bfloat16)

    pltpu.make_async_copy(from_line, from_line, line_send).wait()
    for held, sem in ((rows_in, 0), (cols_in, 1)):
        sent = held.at[pl.ds(0, (plane_count - 1) * grow_count)]
        pltpu.make_async_copy(sent, sent, plane_send.at[sem]).wait()


def on_device(sizes, valence, conduction, val_energy, cond_energy, frequencies, gvec_index, first_band):
    band_count, grow_count, gcol_count = sizes
    devices = band_count * grow_count * gcol_count
    val_count = val_energy.shape[0]
    freq_count = frequencies.shape[0]
    num_gvec = gvec_index.shape[0]
    rows = val_count * GRID
    num_tiles = num_gvec // TILE
    col_tiles = num_tiles // gcol_count
    tile_shape = (4 * val_count, LANES)
    operands = (
        valence,
        conduction,
        jnp.asarray(plane_table()),
        jnp.asarray(phase_table(val_count)),
        gvec_index.reshape(num_tiles, 1, TILE),
        val_energy[None],
        cond_energy[None],
        frequencies[None],
        first_band[None],
    )
    out_shape = (freq_count, 2, TILE, num_gvec // gcol_count)
    out = pl.pallas_call(
        functools.partial(kernel, sizes),
        out_shape=jax.ShapeDtypeStruct(out_shape, jnp.bfloat16),
        in_specs=[pl.BlockSpec(memory_space=pl.ANY)] * len(operands),
        out_specs=pl.BlockSpec(memory_space=pltpu.VMEM),
        scratch_shapes=[
            pltpu.VMEM(valence.shape, jnp.bfloat16),
            pltpu.VMEM(conduction.shape, jnp.bfloat16),
            pltpu.VMEM((2 * CHUNKS, PLANE, CHUNK), jnp.bfloat16),
            *(pltpu.VMEM(operand.shape, operand.dtype) for operand in operands[3:]),
            pltpu.VMEM((2 * rows, PLANE), jnp.bfloat16),
            pltpu.VMEM((4 * rows, CHUNKS * CHUNK), jnp.bfloat16),
            pltpu.VMEM((num_tiles,) + tile_shape, jnp.bfloat16),
            pltpu.VMEM((grow_count - 1, num_tiles) + tile_shape, jnp.bfloat16),
            pltpu.VMEM((devices,) + tile_shape, jnp.bfloat16),
            pltpu.VMEM((devices, col_tiles) + tile_shape, jnp.bfloat16),
            pltpu.SemaphoreType.DMA((len(operands) - 1,)),
            pltpu.SemaphoreType.DMA((2 * CHUNKS,)),
            pltpu.SemaphoreType.DMA,
            pltpu.SemaphoreType.DMA((grow_count - 1,)),
            pltpu.SemaphoreType.DMA((2,)),
            pltpu.SemaphoreType.DMA((2,)),
        ],
        compiler_params=pltpu.CompilerParams(
            collective_id=0, has_side_effects=True, vmem_limit_bytes=63 * 2**20
        ),
    )(*operands)
    out = jnp.transpose(out, (2, 0, 1, 3))
    row_count = num_gvec // (grow_count * band_count)
    if row_count < TILE:
        block = lax.axis_index("grow") * band_count + lax.axis_index("band")
        out = lax.dynamic_slice_in_dim(out, block * row_count % TILE, row_count, 0)
    return out


def solution(mesh):
    sizes = tuple(mesh.shape[name] for name in ("band", "grow", "gcol"))
    return jax.shard_map(
        functools.partial(on_device, sizes),
        mesh=mesh,
        in_specs=(P(), P(("band", "grow", "gcol"), None), P(), P(), P(), P(), P()),
        out_specs=P(("grow", "band"), None, None, "gcol"),
        check_vma=False,
    )
```

time: 40.5 us -> 36.8 us (0.909)
  Pallas kernels: 37.1 us -> 33.4 us
    pallas_call x1, Pallas kernels: 37.1 us -> 33.4 us  [on_device(): pl.pallas_call(functools.partial(kernel, sizes), out_shape=jax.ShapeDtype...]
where the time goes in v3:
time: 36.8 us; the launch traced here: 36.7 us
  Pallas kernels  33.4 us (91%)
  local copies, waits for them, and re-layouts  3.27 us (9%)
    pallas_call x1, Pallas kernels, on_device(): pl.pallas_call(functools.partial(kernel, sizes), out_shape=jax.ShapeDtype...  33.4 us
    transpose x1, local copies, waits for them, and re-layouts, on_device(): out = jnp.transpose(out, (2, 0, 1, 3))  3.27 us

profile of v3, /device:TPU:0, one launch (start us, length us, event | category | flops | bytes accessed | tf_op | source)
XLA Modules:
  0.0 36.7 jit_solution(14337992220310238870)
XLA Ops:
  0.0 33.4 %shard_map.91 = bf16[2,2,256,512]{3,2,1,0:T(8,128)(2,1)} custom-call(bf16[4,110592]{1,0:T(4,128)(2,1)} %val_hbm.1, bf16[1,110592]{1,0:T(2,128)(2,1)} %cond_hbm.1, bf16[10,2304,256]{2,1,0:T(8,128)(2,1)} %constant.4.clone.table_hbm, bf16[384,128]{1,0:T(8,128)(2,1)} %constant.5.clone.phase_hbm, s32[8,1,256]{2,1,0:T(1,128)} %bitcast.7, f32[1,4]{1,0:T(1,128)} %bitcast.8, ...), custom_call_target="tpu_custom_call" | custom-call | tf_op jit(solution)/shard_map/pallas_call | solution.py:285
  33.4 3.3 %copy.10 = bf16[256,2,2,512]{3,2,1,0:T(2,128)(2,1)} copy(bf16[256,2,2,512]{3,0,2,1:T(8,128)(2,1)} %bitcast.6) | data formatting | bytes 2097152 | tf_op jit(solution)/shard_map/transpose | solution.py:312

commit v4 on v3

--- a/solution.py
+++ b/solution.py
@@ -141,11 +141,8 @@
         table_loads[step].wait()
         both = jnp.dot(pair[...], table_ref[step], preferred_element_type=jnp.float32)
         total = both[:rows] + both[rows:]
-        high = total.astype(jnp.bfloat16)
-        start = step // CHUNKS * 2 * rows
-        where = pl.ds(step % CHUNKS * CHUNK, CHUNK)
-        planes[start : start + rows, where] = high
-        planes[start + rows : start + 2 * rows, where] = (total - high.astype(jnp.float32)).astype(jnp.bfloat16)
+        start = step // CHUNKS * rows
+        planes[start : start + rows, pl.ds(step % CHUNKS * CHUNK, CHUNK)] = total.astype(jnp.bfloat16)
 
     for copy in small_loads:
         copy.wait()
@@ -168,8 +165,7 @@
         line = lax.broadcasted_iota(jnp.int32, (CHUNKS * CHUNK, TILE), 0)
         pick = jnp.where(line == place, 1.0, 0.0).astype(jnp.bfloat16)
         picked = jnp.dot(planes[...], pick, preferred_element_type=jnp.float32)
-        real = picked[:rows] + picked[rows : 2 * rows]
-        imag = picked[2 * rows : 3 * rows] + picked[3 * rows :]
+        real, imag = picked[:rows], picked[rows:]
         line = line[:LANES]
         pick = jnp.where((line == k1) | (line == k1 + LANES // 2), 1.0, 0.0).astype(jnp.bfloat16)
         phases = jnp.dot(phase_ref[...], pick, preferred_element_type=jnp.float32)
@@ -242,17 +238,19 @@
          for tile in range(col_tiles) for side in range(2)], 1
     ).astype(jnp.bfloat16)
     inward = rows_in[...].astype(jnp.float32)
-    for side in range(2):
-        part = inward[:, side * half : (side + 1) * half].reshape(depth, LANES)
-        for freq in range(freq_count):
-            left = part * weights[freq]
-            cube = left.reshape(devices, half, LANES)
-            swapped = jnp.concatenate([cube[:, val_count:], -cube[:, :val_count]], 1)
-            for kind, value in enumerate((left, swapped.reshape(depth, LANES))):
-                out_ref[freq, kind, side * LANES : (side + 1) * LANES] = lax.dot_general(
-                    value.astype(jnp.bfloat16), right, (((0,), (0,)), ((), ())),
-                    preferred_element_type=jnp.float32,
-                ).astype(jnp.bfloat16)
+    parts = [inward[:, side * half : (side + 1) * half].reshape(depth, LANES) for side in range(2)]
+    lefts = []
+    for freq in range(freq_count):
+        kept = [part * weights[freq] for part in parts]
+        cubes = [left.reshape(devices, half, LANES) for left in kept]
+        turned_round = [
+            jnp.concatenate([cube[:, val_count:], -cube[:, :val_count]], 1).reshape(depth, LANES) for cube in cubes
+        ]
+        lefts += kept + turned_round
+    left = jnp.concatenate(lefts, 1).astype(jnp.bfloat16)
+    out_ref[...] = lax.dot_general(
+        left, right, (((0,), (0,)), ((), ())), preferred_element_type=jnp.float32
+    ).astype(jnp.bfloat16).reshape(out_ref.shape)
 
     pltpu.make_async_copy(from_line, from_line, line_send).wait()
     for held, sem in ((rows_in, 0), (cols_in, 1)):
@@ -293,7 +291,7 @@
             pltpu.VMEM((2 * CHUNKS, PLANE, CHUNK), jnp.bfloat16),
             *(pltpu.VMEM(operand.shape, operand.dtype) for operand in operands[3:]),
             pltpu.VMEM((2 * rows, PLANE), jnp.bfloat16),
-            pltpu.VMEM((4 * rows, CHUNKS * CHUNK), jnp.bfloat16),
+            pltpu.VMEM((2 * rows, CHUNKS * CHUNK), jnp.bfloat16),
             pltpu.VMEM((num_tiles,) + tile_shape, jnp.bfloat16),
             pltpu.VMEM((grow_count - 1, num_tiles) + tile_shape, jnp.bfloat16),
             pltpu.VMEM((devices,) + tile_shape, jnp.bfloat16),

time: 36.8 us -> 34.6 us (0.940)
  Pallas kernels: 33.4 us -> 31.2 us
    pallas_call x1, Pallas kernels: 33.4 us -> 31.2 us  [on_device(): pl.pallas_call(functools.partial(kernel, sizes), out_shape=jax.ShapeDtype...]
where the time goes in v4:
time: 34.6 us; the launch traced here: 34.4 us
  Pallas kernels  31.2 us (90%)
  local copies, waits for them, and re-layouts  3.27 us (9%)
    pallas_call x1, Pallas kernels, on_device(): pl.pallas_call(functools.partial(kernel, sizes), out_shape=jax.ShapeDtype...  31.2 us
    transpose x1, local copies, waits for them, and re-layouts, on_device(): out = jnp.transpose(out, (2, 0, 1, 3))  3.27 us

profile of v4, /device:TPU:0, one launch (start us, length us, event | category | flops | bytes accessed | tf_op | source)
XLA Modules:
  0.0 34.4 jit_solution(9426155848883753534)
XLA Ops:
  0.0 31.2 %shard_map.91 = bf16[2,2,256,512]{3,2,1,0:T(8,128)(2,1)} custom-call(bf16[4,110592]{1,0:T(4,128)(2,1)} %val_hbm.1, bf16[1,110592]{1,0:T(2,128)(2,1)} %cond_hbm.1, bf16[10,2304,256]{2,1,0:T(8,128)(2,1)} %constant.4.clone.table_hbm, bf16[384,128]{1,0:T(8,128)(2,1)} %constant.5.clone.phase_hbm, s32[8,1,256]{2,1,0:T(1,128)} %bitcast.7, f32[1,4]{1,0:T(1,128)} %bitcast.8, ...), custom_call_target="tpu_custom_call" | custom-call | tf_op jit(solution)/shard_map/pallas_call | solution.py:283
  31.2 3.3 %copy.10 = bf16[256,2,2,512]{3,2,1,0:T(2,128)(2,1)} copy(bf16[256,2,2,512]{3,0,2,1:T(8,128)(2,1)} %bitcast.6) | data formatting | bytes 2097152 | tf_op jit(solution)/shard_map/transpose | solution.py:310

commit v5 on v4

--- a/solution.py
+++ b/solution.py
@@ -17,6 +17,7 @@
 CHUNKS = -(-GRID * HALF // CHUNK)
 TILE = 256
 LANES = 128
+WIDE = 2 * TILE
 MESH = pl.DeviceIdType.MESH
 TABLE_SCALE = 1.622
 TABLE_GAIN = 1.6242055647
@@ -35,8 +36,8 @@
         small = (values * TABLE_SCALE).astype(np.float32).astype(ml_dtypes.bfloat16)
         full = np.zeros((PLANE, CHUNKS * CHUNK), ml_dtypes.bfloat16)
         full[:, : GRID * HALF] = small[turn]
-        parts.append(full.reshape(PLANE, CHUNKS, CHUNK).transpose(1, 0, 2))
-    return np.concatenate(parts, 0)
+        parts.append(full)
+    return np.concatenate(parts, 1).reshape(PLANE, CHUNKS, WIDE).transpose(1, 0, 2)
 
 
 def phase_table(val_count):
@@ -72,7 +73,7 @@
 
     loads = [pltpu.make_async_copy(val_hbm, val_ref, load.at[0]), pltpu.make_async_copy(cond_hbm, cond_ref, load.at[1])]
     table_loads = [
-        pltpu.make_async_copy(table_hbm.at[n], table_ref.at[n], table_load.at[n]) for n in range(2 * CHUNKS)
+        pltpu.make_async_copy(table_hbm.at[n], table_ref.at[n], table_load.at[n]) for n in range(CHUNKS)
     ]
     small_loads = [
         pltpu.make_async_copy(source, target, load.at[2 + n])
@@ -137,18 +138,22 @@
         pair[pl.ds(start, 16)] = high
         pair[pl.ds(rows + start, 16)] = (product - high.astype(jnp.float32)).astype(jnp.bfloat16)
 
-    for step in range(2 * CHUNKS):
+    for step in range(CHUNKS):
         table_loads[step].wait()
         both = jnp.dot(pair[...], table_ref[step], preferred_element_type=jnp.float32)
-        total = both[:rows] + both[rows:]
-        start = step // CHUNKS * rows
-        planes[start : start + rows, pl.ds(step % CHUNKS * CHUNK, CHUNK)] = total.astype(jnp.bfloat16)
+        total = (both[:rows] + both[rows:]).astype(jnp.bfloat16)
+        for side in range(2):
+            number = 2 * step + side
+            start = number // CHUNKS * rows
+            planes[start : start + rows, pl.ds(number % CHUNKS * CHUNK, CHUNK)] = (
+                total[:, side * CHUNK : (side + 1) * CHUNK]
+            )
 
     for copy in small_loads:
         copy.wait()
     pl.semaphore_wait(barrier, grow_count - 1 + plane_count - 1)
 
-    @pl.loop(0, num_tiles)
+    @pl.loop(0, num_tiles // 2)
     def _(tile):
         index = index_ref[tile]
         index_float = index.astype(jnp.float32)
@@ -162,7 +167,7 @@
         k3 = jnp.where(mirror, GRID - k3, k3)
         sign = jnp.where(mirror, -1.0, 1.0)
         place = (k2 * HALF + k3).astype(jnp.int32)
-        line = lax.broadcasted_iota(jnp.int32, (CHUNKS * CHUNK, TILE), 0)
+        line = lax.broadcasted_iota(jnp.int32, (CHUNKS * CHUNK, WIDE), 0)
         pick = jnp.where(line == place, 1.0, 0.0).astype(jnp.bfloat16)
         picked = jnp.dot(planes[...], pick, preferred_element_type=jnp.float32)
         real, imag = picked[:rows], picked[rows:]
@@ -175,15 +180,16 @@
             (real * cos_one + imag * sin_one, None),
             (imag * cos_one - real * sin_one, sign),
         ):
-            value = jnp.sum(value.reshape(rows // 8, 8, TILE), axis=0)
+            value = jnp.sum(value.reshape(rows // 8, 8, WIDE), axis=0)
             value = sum(value[n * val_count : (n + 1) * val_count] for n in range(8 // val_count))
             out.append(value if flip is None else value * flip)
         out = jnp.concatenate(out, 0)
-        out = jnp.concatenate([out[:, :LANES], out[:, LANES:]], 0)
-        tiles[tile] = out.astype(jnp.bfloat16)
+        out = [out[:, n * LANES : (n + 1) * LANES] for n in range(WIDE // LANES)]
+        for side in range(2):
+            tiles[2 * tile + side] = jnp.concatenate(out[2 * side : 2 * side + 2], 0).astype(jnp.bfloat16)
         for offset in range(1, grow_count):
             pltpu.make_async_remote_copy(
-                tiles.at[tile], from_line.at[offset - 1, tile], line_send, line_recv.at[offset - 1],
+                tiles.at[pl.ds(2 * tile, 2)], from_line.at[offset - 1, pl.ds(2 * tile, 2)], line_send, line_recv.at[offset - 1],
                 device_id=line_peer(offset), device_id_type=MESH,
             ).start()
 
@@ -273,7 +279,7 @@
         conduction,
         jnp.asarray(plane_table()),
         jnp.asarray(phase_table(val_count)),
-        gvec_index.reshape(num_tiles, 1, TILE),
+        gvec_index.reshape(num_tiles // 2, 1, WIDE),
         val_energy[None],
         cond_energy[None],
         frequencies[None],
@@ -288,7 +294,7 @@
         scratch_shapes=[
             pltpu.VMEM(valence.shape, jnp.bfloat16),
             pltpu.VMEM(conduction.shape, jnp.bfloat16),
-            pltpu.VMEM((2 * CHUNKS, PLANE, CHUNK), jnp.bfloat16),
+            pltpu.VMEM((CHUNKS, PLANE, WIDE), jnp.bfloat16),
             *(pltpu.VMEM(operand.shape, operand.dtype) for operand in operands[3:]),
             pltpu.VMEM((2 * rows, PLANE), jnp.bfloat16),
             pltpu.VMEM((2 * rows, CHUNKS * CHUNK), jnp.bfloat16),
@@ -297,7 +303,7 @@
             pltpu.VMEM((devices,) + tile_shape, jnp.bfloat16),
             pltpu.VMEM((devices, col_tiles) + tile_shape, jnp.bfloat16),
             pltpu.SemaphoreType.DMA((len(operands) - 1,)),
-            pltpu.SemaphoreType.DMA((2 * CHUNKS,)),
+            pltpu.SemaphoreType.DMA((CHUNKS,)),
             pltpu.SemaphoreType.DMA,
             pltpu.SemaphoreType.DMA((grow_count - 1,)),
             pltpu.SemaphoreType.DMA((2,)),

time: 34.6 us -> 29.3 us (0.85)
  Pallas kernels: 31.2 us -> 25.8 us
    pallas_call x1, Pallas kernels: 31.2 us -> 25.8 us  [on_device(): pl.pallas_call(functools.partial(kernel, sizes), out_shape=jax.ShapeDtype...]
where the time goes in v5:
time: 29.3 us; the launch traced here: 29.1 us
  Pallas kernels  25.8 us (88%)
  local copies, waits for them, and re-layouts  3.27 us (11%)
    pallas_call x1, Pallas kernels, on_device(): pl.pallas_call(functools.partial(kernel, sizes), out_shape=jax.ShapeDtype...  25.8 us
    transpose x1, local copies, waits for them, and re-layouts, on_device(): out = jnp.transpose(out, (2, 0, 1, 3))  3.27 us

profile of v5, /device:TPU:0, one launch (start us, length us, event | category | flops | bytes accessed | tf_op | source)
XLA Modules:
  0.0 29.1 jit_solution(4976618706934955330)
XLA Ops:
  0.0 25.8 %shard_map.91 = bf16[2,2,256,512]{3,2,1,0:T(8,128)(2,1)} custom-call(bf16[4,110592]{1,0:T(4,128)(2,1)} %val_hbm.1, bf16[1,110592]{1,0:T(2,128)(2,1)} %cond_hbm.1, bf16[5,2304,512]{2,1,0:T(8,128)(2,1)} %constant.4.clone.table_hbm, bf16[384,128]{1,0:T(8,128)(2,1)} %constant.5.clone.phase_hbm, s32[4,1,512]{2,1,0:T(1,128)} %bitcast.7, f32[1,4]{1,0:T(1,128)} %bitcast.8, ...), custom_call_target="tpu_custom_call" | custom-call | tf_op jit(solution)/shard_map/pallas_call | solution.py:289
  25.8 3.3 %copy.10 = bf16[256,2,2,512]{3,2,1,0:T(2,128)(2,1)} copy(bf16[256,2,2,512]{3,0,2,1:T(8,128)(2,1)} %bitcast.6) | data formatting | bytes 2097152 | tf_op jit(solution)/shard_map/transpose | solution.py:316

commit v6 on v5

--- a/solution.py
+++ b/solution.py
@@ -67,7 +67,7 @@
     rows = val_count * GRID
     num_tiles = tiles.shape[0]
     col_tiles = num_tiles // gcol_count
-    freq_count = out_ref.shape[0]
+    freq_count = frequencies.shape[1]
     band, grow, gcol = (lax.axis_index(name) for name in ("band", "grow", "gcol"))
     barrier = pltpu.get_barrier_semaphore()
 
@@ -244,19 +244,24 @@
          for tile in range(col_tiles) for side in range(2)], 1
     ).astype(jnp.bfloat16)
     inward = rows_in[...].astype(jnp.float32)
-    parts = [inward[:, side * half : (side + 1) * half].reshape(depth, LANES) for side in range(2)]
-    lefts = []
-    for freq in range(freq_count):
-        kept = [part * weights[freq] for part in parts]
-        cubes = [left.reshape(devices, half, LANES) for left in kept]
-        turned_round = [
-            jnp.concatenate([cube[:, val_count:], -cube[:, :val_count]], 1).reshape(depth, LANES) for cube in cubes
-        ]
-        lefts += kept + turned_round
-    left = jnp.concatenate(lefts, 1).astype(jnp.bfloat16)
+    inward = jnp.concatenate(
+        [inward[:, side * half : (side + 1) * half].reshape(depth, LANES) for side in range(2)], 1
+    ).astype(jnp.bfloat16)
+    wide = out_ref.shape[0]
+    copies = wide // TILE
+    lane = lax.broadcasted_iota(jnp.int32, (TILE, wide), 1)
+    repeat = jnp.where(lane // copies == lax.broadcasted_iota(jnp.int32, (TILE, wide), 0), 1.0, 0.0)
+    left = jnp.dot(inward, repeat.astype(jnp.bfloat16), preferred_element_type=jnp.float32)
+    lane = lax.broadcasted_iota(jnp.int32, (1, wide), 1)
+    weight = weights[0]
+    for freq in range(1, freq_count):
+        weight = jnp.where(lane // 2 % freq_count == freq, weights[freq], weight)
+    cube = (left * weight).reshape(devices, half, wide)
+    swapped = jnp.concatenate([cube[:, val_count:], -cube[:, :val_count]], 1)
+    left = jnp.where((lane % 2 == 1)[None], swapped, cube).reshape(depth, wide).astype(jnp.bfloat16)
     out_ref[...] = lax.dot_general(
         left, right, (((0,), (0,)), ((), ())), preferred_element_type=jnp.float32
-    ).astype(jnp.bfloat16).reshape(out_ref.shape)
+    ).astype(jnp.bfloat16)
 
     pltpu.make_async_copy(from_line, from_line, line_send).wait()
     for held, sem in ((rows_in, 0), (cols_in, 1)):
@@ -285,7 +290,7 @@
         frequencies[None],
         first_band[None],
     )
-    out_shape = (freq_count, 2, TILE, num_gvec // gcol_count)
+    out_shape = (TILE * freq_count * 2, num_gvec // gcol_count)
     out = pl.pallas_call(
         functools.partial(kernel, sizes),
         out_shape=jax.ShapeDtypeStruct(out_shape, jnp.bfloat16),
@@ -313,7 +318,7 @@
             collective_id=0, has_side_effects=True, vmem_limit_bytes=63 * 2**20
         ),
     )(*operands)
-    out = jnp.transpose(out, (2, 0, 1, 3))
+    out = out.reshape(TILE, freq_count, 2, num_gvec // gcol_count)
     row_count = num_gvec // (grow_count * band_count)
     if row_count < TILE:
         block = lax.axis_index("grow") * band_count + lax.axis_index("band")

time: 29.3 us -> 28.4 us (0.969)
  local copies, waits for them, and re-layouts: 3.27 us -> 2.25 us
    transpose x1 -> x0, local copies, waits for them, and re-layouts: 3.27 us -> none  [on_device(): out = jnp.transpose(out, (2, 0, 1, 3))]
    reshape x0 -> x1, local copies, waits for them, and re-layouts: none -> 2.25 us  [on_device(): out = out.reshape(TILE, freq_count, 2, num_gvec // gcol_count)]
where the time goes in v6:
time: 28.4 us; the launch traced here: 28.2 us
  Pallas kernels  26 us (92%)
  local copies, waits for them, and re-layouts  2.25 us (8%)
    pallas_call x1, Pallas kernels, on_device(): pl.pallas_call(functools.partial(kernel, sizes), out_shape=jax.ShapeDtype...  26 us
    reshape x1, local copies, waits for them, and re-layouts, on_device(): out = out.reshape(TILE, freq_count, 2, num_gvec // gcol_count)  2.25 us

profile of v6, /device:TPU:0, one launch (start us, length us, event | category | flops | bytes accessed | tf_op | source)
XLA Modules:
  0.0 28.2 jit_solution(3484241199420411932)
XLA Ops:
  0.0 26.0 %shard_map.91 = bf16[1024,512]{1,0:T(8,128)(2,1)} custom-call(bf16[4,110592]{1,0:T(4,128)(2,1)} %val_hbm.1, bf16[1,110592]{1,0:T(2,128)(2,1)} %cond_hbm.1, bf16[5,2304,512]{2,1,0:T(8,128)(2,1)} %constant.4.clone.table_hbm, bf16[384,128]{1,0:T(8,128)(2,1)} %constant.5.clone.phase_hbm, s32[4,1,512]{2,1,0:T(1,128)} %bitcast.5, f32[1,4]{1,0:T(1,128)} %bitcast.6, ...), custom_call_target="tpu_custom_call" | custom-call | tf_op jit(solution)/shard_map/pallas_call | solution.py:294
  26.0 2.2 %reshape.7 = bf16[256,2,2,512]{3,2,1,0:T(2,128)(2,1)} reshape(bf16[1024,512]{1,0:T(8,128)(2,1)} %shard_map.91) | data formatting | bytes 2097152 | tf_op jit(solution)/shard_map/reshape | solution.py:321

commit v7 on v6

--- a/solution.py
+++ b/solution.py
@@ -153,7 +153,41 @@
         copy.wait()
     pl.semaphore_wait(barrier, grow_count - 1 + plane_count - 1)
 
-    @pl.loop(0, num_tiles // 2)
+    here = (band, grow, gcol)
+    pair_count = num_tiles // 2
+
+    def send(source, target, sem, place):
+        pltpu.make_async_remote_copy(
+            source, target, plane_send.at[sem], plane_recv.at[sem], device_id=place, device_id_type=MESH
+        ).start()
+
+    def spread(source, origin, number):
+        columns = source.at[pl.ds(number * col_tiles, col_tiles)]
+
+        @pl.when(number == gcol)
+        def _():
+            pltpu.make_async_copy(columns, cols_in.at[origin], plane_recv.at[1]).start()
+
+        @pl.when(number != gcol)
+        def _():
+            send(columns, cols_in.at[origin], 1, (band, grow, number))
+
+        for offset in range(1, band_count):
+            send(columns, cols_in.at[origin], 1, (turned(band, offset, band_count), grow, number))
+
+        @pl.when(number == grow)
+        def _():
+            pltpu.make_async_copy(source.at[row_tile(here)], rows_in.at[origin], plane_recv.at[0]).start()
+            each_plane_peer(lambda place: send(source.at[row_tile(place)], rows_in.at[origin], 0, place))
+
+    def forward(number):
+        for offset in range(1, grow_count):
+            arrived = from_line.at[offset - 1]
+            part = arrived.at[pl.ds(2 * number, 2)]
+            pltpu.make_async_copy(part, part, line_recv.at[offset - 1, number]).wait()
+            spread(arrived, number_of(line_peer(grow_count - offset)), number)
+
+    @pl.loop(0, pair_count)
     def _(tile):
         index = index_ref[tile]
         index_float = index.astype(jnp.float32)
@@ -189,34 +223,13 @@
             tiles[2 * tile + side] = jnp.concatenate(out[2 * side : 2 * side + 2], 0).astype(jnp.bfloat16)
         for offset in range(1, grow_count):
             pltpu.make_async_remote_copy(
-                tiles.at[pl.ds(2 * tile, 2)], from_line.at[offset - 1, pl.ds(2 * tile, 2)], line_send, line_recv.at[offset - 1],
+                tiles.at[pl.ds(2 * tile, 2)], from_line.at[offset - 1, pl.ds(2 * tile, 2)], line_send, line_recv.at[offset - 1, tile],
                 device_id=line_peer(offset), device_id_type=MESH,
             ).start()
-
-    def spread(source, origin):
-        def send(place):
-            pltpu.make_async_remote_copy(
-                source.at[row_tile(place)], rows_in.at[origin], plane_send.at[0], plane_recv.at[0],
-                device_id=place, device_id_type=MESH,
-            ).start()
-            pltpu.make_async_remote_copy(
-                source.at[pl.ds(place[2] * col_tiles, col_tiles)], cols_in.at[origin],
-                plane_send.at[1], plane_recv.at[1],
-                device_id=place, device_id_type=MESH,
-            ).start()
-
-        each_plane_peer(send)
-        place = (band, grow, gcol)
-        pltpu.make_async_copy(source.at[row_tile(place)], rows_in.at[origin], plane_recv.at[0]).start()
-        pltpu.make_async_copy(
-            source.at[pl.ds(gcol * col_tiles, col_tiles)], cols_in.at[origin], plane_recv.at[1]
-        ).start()
-
-    spread(tiles, number_of((band, grow, gcol)))
-    for offset in range(1, grow_count):
-        arrived = from_line.at[offset - 1]
-        pltpu.make_async_copy(arrived, arrived, line_recv.at[offset - 1]).wait()
-        spread(arrived, number_of(line_peer(grow_count - offset)))
+        spread(tiles, number_of(here), tile)
+        pl.when(tile >= 1)(lambda: forward(tile - 1))
+
+    forward(pair_count - 1)
 
     half = 2 * val_count
     depth = devices * half
@@ -310,7 +323,7 @@
             pltpu.SemaphoreType.DMA((len(operands) - 1,)),
             pltpu.SemaphoreType.DMA((CHUNKS,)),
             pltpu.SemaphoreType.DMA,
-            pltpu.SemaphoreType.DMA((grow_count - 1,)),
+            pltpu.SemaphoreType.DMA((grow_count - 1, num_tiles // 2)),
             pltpu.SemaphoreType.DMA((2,)),
             pltpu.SemaphoreType.DMA((2,)),
         ],

time: 28.4 us -> 27.4 us (0.965)
  the two profiles are of different devices: /device:TPU:0 before, /device:TPU:25 now
where the time goes in v7:
time: 27.4 us; the launch traced here: 27.2 us
  Pallas kernels  25 us (91%)
  local copies, waits for them, and re-layouts  2.25 us (8%)
    pallas_call x1, Pallas kernels, on_device(): pl.pallas_call(functools.partial(kernel, sizes), out_shape=jax.ShapeDtype...  25 us
    reshape x1, local copies, waits for them, and re-layouts, on_device(): out = out.reshape(TILE, freq_count, 2, num_gvec // gcol_count)  2.25 us

profile of v7, /device:TPU:25, one launch (start us, length us, event | category | flops | bytes accessed | tf_op | source)
XLA Modules:
  0.0 27.2 jit_solution(5249049140275002258)
XLA Ops:
  0.0 25.0 %shard_map.91 = bf16[1024,512]{1,0:T(8,128)(2,1)} custom-call(bf16[4,110592]{1,0:T(4,128)(2,1)} %val_hbm.1, bf16[1,110592]{1,0:T(2,128)(2,1)} %cond_hbm.1, bf16[5,2304,512]{2,1,0:T(8,128)(2,1)} %constant.4.clone.table_hbm, bf16[384,128]{1,0:T(8,128)(2,1)} %constant.5.clone.phase_hbm, s32[4,1,512]{2,1,0:T(1,128)} %bitcast.5, f32[1,4]{1,0:T(1,128)} %bitcast.6, ...), custom_call_target="tpu_custom_call" | custom-call | tf_op jit(solution)/shard_map/pallas_call | solution.py:307
  25.0 2.2 %reshape.7 = bf16[256,2,2,512]{3,2,1,0:T(2,128)(2,1)} reshape(bf16[1024,512]{1,0:T(8,128)(2,1)} %shard_map.91) | data formatting | bytes 2097152 | tf_op jit(solution)/shard_map/reshape | solution.py:334
